TPU v7x, 256 devices: a whole 4x4x8 slice. The times are simulated.
256 devices in a mesh: sec: 2 (over z_hi), gx: 32 (over y, x, core), gz: 4 (over z_lo).
Axes of the slice: x: 4, y: 4, z: 8 (z_hi: 2, z_lo: 4; z = z_hi * 4 + z_lo), core: 2. Of those that a mesh axis runs over, the one named last changes fastest.
Arguments:
- velocity: float32 [2, 3, 1024, 32, 512], P('sec', None, 'gx', 'gz'), may hold values from -6 to 6
- drag: float32 [2, 1024, 32, 512], P('sec', 'gx', 'gz'), may hold values from 0.2 to 2
- stream_gain: float32 [513], replicated, may hold values from 0.5 to 2
- span_gain: float32 [257], replicated, may hold values from 0.5 to 2
Outputs:
- advanced: float32 [2, 3, 1024, 32, 512], P('sec', None, 'gx', 'gz')
All inputs are finite; a program needn't handle non-finite values.
Results may differ from a plain program's by a relative error of at most 0.00005.
Values sent between devices are 32-bit elements; how exact they have to be, the bound alone decides.
A program may use at most 128 MiB of HBM per device.

v0:
```python
import jax
import jax.numpy as jnp
from jax import lax
from jax.sharding import PartitionSpec as P

fringe_peak = 4.0
time_step = 0.05


def extended(cells, sides, width):
    for axis, dim in sides:
        count = lax.axis_size(axis)
        ends = count - 1
        head = lax.slice_in_dim(cells, 0, width, axis=dim)
        tail = lax.slice_in_dim(cells, cells.shape[dim] - width, cells.shape[dim], axis=dim)
        cells = jnp.concatenate(
            [
                lax.ppermute(tail, axis, [(i, (i + 1) % count) for i in range(ends)]),
                cells,
                lax.ppermute(head, axis, [((i + 1) % count, i) for i in range(ends)]),
            ],
            axis=dim,
        )
    return cells


def from_behind(x, axis, by):
    peers = lax.axis_size(axis)
    pairs = [(i, i + by) for i in range(peers) if 0 <= i + by < peers]
    return lax.ppermute(x, axis, pairs)


def kernel_table(gains, length):
    half = length // 2
    shifts = lax.broadcasted_iota(jnp.int32, (length, half), 0)
    modes = lax.broadcasted_iota(jnp.int32, (length, half), 1)
    phases = (shifts * modes % length).astype(jnp.float32) * (2.0 * jnp.pi / length)
    wavenum = jnp.arange(half, dtype=jnp.float32) * (2.0 * jnp.pi / length)
    weights = gains[:half] * wavenum
    kernel = -(2.0 / length) * jnp.dot(jnp.sin(phases), weights, precision=lax.Precision.HIGHEST)
    flipped = jnp.concatenate([kernel[:1], kernel[1:][::-1]])
    leading = jnp.tile(flipped, length)[: length * (length - 1)].reshape(length, length - 1)
    return jnp.concatenate([leading, flipped[::-1][:, None]], axis=1)


def fringe_profile(anchor, number, total):
    cells = anchor + jnp.arange(number, dtype=jnp.int32)
    fringe_start = 3 * total // 4
    fringe_width = total // 4
    phases = (cells - fringe_start).astype(jnp.float32) + 0.5
    return jnp.where(
        cells >= fringe_start, fringe_peak * jnp.sin(jnp.pi * phases / fringe_width) ** 2, 0.0
    )


def shards(velocity, drag, stream_gain, span_gain):
    start_fields = velocity[0]
    drag_here = drag[0]
    cells_x = start_fields.shape[1]
    width_y = start_fields.shape[3]
    groups = lax.axis_size("gx")
    total_x = cells_x * groups
    table_x = kernel_table(stream_gain, total_x)
    table_y = kernel_table(span_gain, width_y)
    is_farm = (lax.axis_index("sec") == 1).astype(jnp.float32)

    def tendency(fields):
        block_shape = fields.shape
        flat_block = fields.reshape(3, cells_x, -1)
        pencils = lax.all_to_all(flat_block, "gx", split_axis=2, concat_axis=1, tiled=True)
        gradient = jnp.stack(
            [jnp.dot(table_x, pencils[comp], precision=lax.Precision.HIGHEST) for comp in range(3)]
        )
        returned = lax.all_to_all(gradient, "gx", split_axis=1, concat_axis=2, tiled=True).reshape(
            block_shape
        )
        grad_y = jnp.dot(
            fields.reshape(-1, width_y), table_y.T, precision=lax.Precision.HIGHEST
        ).reshape(block_shape)
        padded = extended(fields, (("gz", 2),), 1)
        grad_z = 0.5 * (padded[:, :, 2:] - padded[:, :, :-2])
        resist = -drag_here[None] * jnp.abs(fields[0:1]) * fields
        upstream = from_behind(fields, "sec", 1)
        profile = fringe_profile(lax.axis_index("gx") * cells_x, cells_x, total_x)
        relax = is_farm * profile[None, :, None, None] * (upstream - fields)
        advect = fields[0:1] * returned + fields[1:2] * grad_y + fields[2:3] * grad_z
        return -advect + resist + relax

    first = start_fields + time_step * tendency(start_fields)
    advanced = 0.5 * start_fields + 0.5 * (first + time_step * tendency(first))
    return advanced[None]


def solution(mesh):
    placed = (P("sec", None, "gx", "gz", None), P("sec", "gx", "gz", None), P(), P())
    return jax.shard_map(
        shards,
        mesh=mesh,
        in_specs=placed,
        out_specs=P("sec", None, "gx", "gz", None),
        check_vma=False,
    )
```

profile of v0, /device:TPU:1, one launch (start us, length us, event | category | flops | bytes accessed | tf_op | source)
XLA Modules:
  0.0 274.4 jit_solution(14216303080541916364)
XLA Ops:
  0.0 6.1 %copy.25 = f32[1,3,32,8,512]{2,1,4,3,0:T(4,128)} copy(f32[1,3,32,8,512]{4,3,2,1,0:T(8,128)} %param.4) | data formatting | bytes 3145728 | tf_op args[0]
  6.1 9.3 %reshape.91 = f32[32,1,12288]{2,1,0:T(1,128)} reshape(f32[4096,3,32]{2,1,0:T(4,128)} %bitcast.97) | data formatting | bytes 3145728
  15.4 8.8 %all-to-all-start = ((f32[32,1,12288]{2,1,0:T(1,128)}), f32[32,1,12288]{2,1,0:T(1,128)}, u32[]{:S(2)}, u32[]{:S(2)}) async-start(f32[32,1,12288]{2,1,0:T(1,128)} %reshape.91), calls=%async_computation | async-start | bytes 3145728 | tf_op jit(solution)/shard_map/all_to_all | solution.py:70
  24.2 10.0 %collective-permute-start.2 = (f32[3,32,8,512]{3,2,1,0:T(8,128)S(1)}, f32[3,32,8,512]{3,2,1,0:T(8,128)}, u32[]{:S(2)}, u32[]{:S(2)}) collective-permute-start(f32[3,32,8,512]{3,2,1,0:T(8,128)S(1)} %bitcast.91), channel_id=1, source_target_pairs={{0,128},{1,129},{2,130},{3,131},{4,132},{5,133},{6,134},{7,135},{8... | collective-permute-start | bytes 4718600 | tf_op jit(solution)/shard_map/ppermute | solution.py:30
  36.4 4.9 %collective-permute-start.1 = (f32[3,32,1,512]{3,2,1,0:T(1,128)}, f32[3,32,1,512]{3,2,1,0:T(1,128)}, u32[]{:S(2)}, u32[]{:S(2)}) collective-permute-start(f32[3,32,1,512]{3,2,1,0:T(1,128)} %get-tuple-element.21), channel_id=1, source_target_pairs={{0,1},{1,2},{2,3},{4,5},{5,6},{6,7},{8,9},{9,10},{10,11},{12,13},{... | collective-permute-start | bytes 589832 | tf_op jit(solution)/shard_map/ppermute | solution.py:18
  41.4 10.4 %fusion.4 = f32[1,1024]{1,0:T(1,128)S(1)} fusion(f32[512,1]{0,1:T(1,128)S(1)} %bitcast.116), kind=kOutput, calls=%fused_computation.8 | convolution fusion | flops 13631488 | bytes 6144 | tf_op jit(solution)/shard_map/dot_general | solution.py:40
  56.0 8.6 %reshape.80 = f32[1024,1023]{1,0:T(8,128)} reshape(f32[1023,1024]{1,0:T(8,128)} %slice.105) | data formatting | bytes 8380416 | tf_op jit(solution)/shard_map/reshape | solution.py:42
  65.3 6.8 %reduce = f32[32,12288]{1,0:T(8,128)} reduce(f32[32,1,12288]{2,1,0:T(1,128)} %all-to-all-done, f32[]{:T(128)} %broadcast.102), dimensions={1}, to_apply=%all_to_all.44.reduce_sub_computation | reduce | bytes 3145732 | tf_op jit(solution)/shard_map/all_to_all | solution.py:70
  72.1 7.8 %reshape.92 = f32[4096,3,32]{2,1,0:T(4,128)} reshape(f32[32,12288]{1,0:T(8,128)} %reduce) | data formatting | bytes 3145728
  79.9 6.4 %copy.42 = f32[3,32,32,128]{3,2,1,0:T(8,128)} copy(f32[3,32,32,128]{1,0,3,2:T(4,128)} %bitcast.95) | data formatting | bytes 3145728 | tf_op jit(solution)/shard_map/all_to_all | solution.py:70
  89.0 3.4 %convolution_bitcast_fusion.4 = f32[1,1024,128]{2,1,0:T(8,128)S(1)} fusion(f32[1024,128]{1,0:T(8,128)S(1)} %bitcast.104, f32[1024,1]{1,0:T(8,128)S(1)} %copy.24, f32[1024,1023]{1,0:T(8,128)S(1)} %copy-done), kind=kOutput, calls=%fused_computation.43 | convolution fusion | flops 1611661312 | bytes 5242880 | tf_op jit(solution)/shard_map/dot_general | solution.py:72
  92.4 3.4 %convolution_bitcast_fusion.5 = f32[1,1024,128]{2,1,0:T(8,128)S(1)} fusion(f32[1024,128]{1,0:T(8,128)S(1)} %bitcast.105, f32[1024,1]{1,0:T(8,128)S(1)} %copy.24, f32[1024,1023]{1,0:T(8,128)S(1)} %copy-done), kind=kOutput, calls=%fused_computation.44 | convolution fusion | flops 1611661312 | bytes 5242880 | tf_op jit(solution)/shard_map/dot_general | solution.py:72
  96.2 3.4 %convolution_bitcast_fusion.6 = f32[1,1024,128]{2,1,0:T(8,128)S(1)} fusion(f32[1024,128]{1,0:T(8,128)S(1)} %bitcast.107, f32[1024,1]{1,0:T(8,128)S(1)} %copy.24, f32[1024,1023]{1,0:T(8,128)S(1)} %copy-done), kind=kOutput, calls=%fused_computation.45 | convolution fusion | flops 1611661312 | bytes 5242880 | tf_op jit(solution)/shard_map/dot_general | solution.py:72
  102.3 8.4 %all-to-all-start.1 = ((f32[3,1024,128]{2,0,1:T(4,128)}), f32[3,1024,128]{2,0,1:T(4,128)}, u32[]{:S(2)}, u32[]{:S(2)}) async-start(f32[3,1024,128]{2,0,1:T(4,128)} %copy.30), calls=%async_computation.1 | async-start | bytes 4194304 | tf_op jit(solution)/shard_map/all_to_all | solution.py:74
  118.3 3.9 %convolution_bitcast_fusion = f32[768,512]{0,1:T(8,128)} fusion(f32[768,512]{1,0:T(8,128)S(1)} %bitcast.93, f32[512,1]{1,0:T(8,128)S(1)} %copy.32, f32[512,511]{1,0:T(8,128)S(1)} %reshape.82), kind=kOutput, calls=%fused_computation.39 | convolution fusion | flops 2416181248 | bytes 4194304 | tf_op jit(solution)/shard_map/dot_general | solution.py:77
  127.5 11.1 %all-to-all-done.1 = f32[3,1024,128]{2,0,1:T(4,128)} async-done(((f32[3,1024,128]{2,0,1:T(4,128)}), f32[3,1024,128]{2,0,1:T(4,128)}, u32[]{:S(2)}, u32[]{:S(2)}) %all-to-all-start.1) | async-done | bytes 1572896 | tf_op jit(solution)/shard_map/all_to_all | solution.py:74
  142.5 4.3 %fusion.28 = f32[3,32,8,512]{3,2,1,0:T(8,128)S(1)} fusion(f32[3,32,8,512]{3,2,1,0:T(8,128)S(1)} %bitcast.94, f32[3,32,1,512]{3,2,1,0:T(1,128)} %collective-permute-done.1, f32[3,32,1,512]{3,2,1,0:T(1,128)} %collective-permute-done, f32[3,32,8,512]{3,2,1,0:T(8,128)} %collective-permute-done.2, f32[3,32,8,512]{3,2,1,0:T(8,128)} %bitcast.103, ...), kind=kLoop, calls=%fused_computation.33 | loop fusion | flops 6291456 | bytes 10354816 | tf_op jit(solution)/shard_map/add | solution.py:89
  146.8 4.7 %copy.43 = f32[3,32,8,512]{1,0,3,2:T(4,128)} copy(f32[3,32,8,512]{3,2,1,0:T(8,128)S(1)} %fusion.28) | data formatting | bytes 3145728 | tf_op jit(solution)/shard_map/reshape | solution.py:69
  151.5 9.3 %reshape.93 = f32[32,1,12288]{2,1,0:T(1,128)} reshape(f32[4096,3,32]{2,1,0:T(4,128)} %bitcast.98) | data formatting | bytes 3145728
  160.8 6.7 %all-to-all-start.2 = ((f32[32,1,12288]{2,1,0:T(1,128)}), f32[32,1,12288]{2,1,0:T(1,128)}, u32[]{:S(2)}, u32[]{:S(2)}) async-start(f32[32,1,12288]{2,1,0:T(1,128)} %reshape.93), calls=%async_computation.2 | async-start | bytes 3145728 | tf_op jit(solution)/shard_map/all_to_all | solution.py:70
  169.9 19.8 %all-to-all-done.2 = f32[32,1,12288]{2,1,0:T(1,128)} async-done(((f32[32,1,12288]{2,1,0:T(1,128)}), f32[32,1,12288]{2,1,0:T(1,128)}, u32[]{:S(2)}, u32[]{:S(2)}) %all-to-all-start.2) | async-done | bytes 1572896 | tf_op jit(solution)/shard_map/all_to_all | solution.py:70
  189.7 6.8 %reduce.1 = f32[32,12288]{1,0:T(8,128)} reduce(f32[32,1,12288]{2,1,0:T(1,128)} %all-to-all-done.2, f32[]{:T(128)} %broadcast.102), dimensions={1}, to_apply=%all_to_all.50.reduce_sub_computation | reduce | bytes 3145732 | tf_op jit(solution)/shard_map/all_to_all | solution.py:70
  196.6 7.8 %reshape.94 = f32[4096,3,32]{2,1,0:T(4,128)} reshape(f32[32,12288]{1,0:T(8,128)} %reduce.1) | data formatting | bytes 3145728
  204.3 6.2 %copy.44 = f32[3,32,32,128]{3,2,1,0:T(8,128)} copy(f32[3,32,32,128]{1,0,3,2:T(4,128)} %bitcast.96) | data formatting | bytes 3145728 | tf_op jit(solution)/shard_map/all_to_all | solution.py:70
  213.2 4.5 %convolution_bitcast_fusion.3 = f32[1,1024,128]{2,1,0:T(8,128)S(1)} fusion(f32[1024,128]{1,0:T(8,128)S(1)} %bitcast.108, f32[1024,1]{1,0:T(8,128)} %copy-done.3, f32[1024,1023]{1,0:T(8,128)S(1)} %copy-done.1), kind=kOutput, calls=%fused_computation.42 | convolution fusion | flops 1611661312 | bytes 5242880 | tf_op jit(solution)/shard_map/dot_general | solution.py:72
  218.1 3.4 %convolution_bitcast_fusion.2 = f32[1,1024,128]{2,1,0:T(8,128)S(1)} fusion(f32[1024,128]{1,0:T(8,128)S(1)} %bitcast.109, f32[1024,1]{1,0:T(8,128)S(1)} %copy-done.4, f32[1024,1023]{1,0:T(8,128)S(1)} %copy-done.1), kind=kOutput, calls=%fused_computation.41 | convolution fusion | flops 1611661312 | bytes 5242880 | tf_op jit(solution)/shard_map/dot_general | solution.py:72
  227.9 6.4 %all-to-all-start.3 = ((f32[3,1024,128]{2,0,1:T(4,128)}), f32[3,1024,128]{2,0,1:T(4,128)}, u32[]{:S(2)}, u32[]{:S(2)}) async-start(f32[3,1024,128]{2,0,1:T(4,128)} %copy.39), calls=%async_computation.3 | async-start | bytes 4194304 | tf_op jit(solution)/shard_map/all_to_all | solution.py:74
  236.7 4.8 %collective-permute-start.4 = (f32[3,32,1,512]{3,2,1,0:T(1,128)}, f32[3,32,1,512]{3,2,1,0:T(1,128)}, u32[]{:S(2)}, u32[]{:S(2)}) collective-permute-start(f32[3,32,1,512]{3,2,1,0:T(1,128)} %get-tuple-element.13), channel_id=1, source_target_pairs={{0,1},{1,2},{2,3},{4,5},{5,6},{6,7},{8,9},{9,10},{10,11},{12,13},{... | collective-permute-start | bytes 589832 | tf_op jit(solution)/shard_map/ppermute | solution.py:18
  241.5 5.1 %fusion.29 = f32[3,32,8,512]{3,2,1,0:T(8,128)} fusion(f32[3,32,8,512]{3,2,1,0:T(8,128)S(1)} %fusion.28, f32[512,1]{1,0:T(8,128)S(1)} %copy.32, f32[512,511]{1,0:T(8,128)} %copy-done.5), kind=kOutput, calls=%fused_computation.47 | convolution fusion | flops 2416181248 | bytes 4194304 | tf_op jit(solution)/shard_map/dot_general | solution.py:77
  248.0 14.4 %all-to-all-done.3 = f32[3,1024,128]{2,0,1:T(4,128)} async-done(((f32[3,1024,128]{2,0,1:T(4,128)}), f32[3,1024,128]{2,0,1:T(4,128)}, u32[]{:S(2)}, u32[]{:S(2)}) %all-to-all-start.3) | async-done | bytes 1572896 | tf_op jit(solution)/shard_map/all_to_all | solution.py:74
  262.3 3.6 %copy.47 = f32[3,32,32,128]{3,1,2,0:T(8,128)} copy(f32[3,32,32,128]{3,0,2,1:T(4,128)} %bitcast.36) | data formatting | bytes 3145728 | tf_op jit(solution)/shard_map/all_to_all | solution.py:74
  268.6 5.6 %fusion.20 = f32[1,3,32,8,512]{4,3,2,1,0:T(8,128)} fusion(f32[3,32,8,512]{3,2,1,0:T(8,128)S(1)} %fusion.28, f32[3,32,1,512]{3,2,1,0:T(1,128)} %collective-permute-done.4, f32[3,32,1,512]{3,2,1,0:T(1,128)} %collective-permute-done.3, f32[3,32,8,512]{3,2,1,0:T(8,128)} %collective-permute-done.5, f32[3,32,8,512]{3,2,1,0:T(8,128)} %fusion.29, ...), kind=kLoop, calls=%fused_computation.23 | loop fusion | flops 7077888 | bytes 11927680 | tf_op jit(solution)/shard_map/broadcast_in_dim | solution.py:91
  (76 shorter events, 47.7 us)
Async XLA Ops:
  15.4 8.8 %copy-start.2 = (f32[1,3,32,8,512]{4,3,2,1,0:T(8,128)S(1)}, f32[1,3,32,8,512]{4,3,2,1,0:T(8,128)}, u32[]{:S(2)}) copy-start(f32[1,3,32,8,512]{4,3,2,1,0:T(8,128)} %param.4) | copy-start | bytes 4718596
  15.4 26.0 %copy-start.8 = (f32[513]{0:T(1024)S(1)}, f32[513]{0:T(1024)}, u32[]{:S(2)}) copy-start(f32[513]{0:T(1024)} %param.6) | copy-start | bytes 6160
  15.4 49.4 %all-to-all-start = ((f32[32,1,12288]{2,1,0:T(1,128)}), f32[32,1,12288]{2,1,0:T(1,128)}, u32[]{:S(2)}, u32[]{:S(2)}) async-start(f32[32,1,12288]{2,1,0:T(1,128)} %reshape.91), calls=%async_computation | async-start | bytes 3145728 | tf_op jit(solution)/shard_map/all_to_all | solution.py:70
  24.2 118.3 %collective-permute-start.2 = (f32[3,32,8,512]{3,2,1,0:T(8,128)S(1)}, f32[3,32,8,512]{3,2,1,0:T(8,128)}, u32[]{:S(2)}, u32[]{:S(2)}) collective-permute-start(f32[3,32,8,512]{3,2,1,0:T(8,128)S(1)} %bitcast.91), channel_id=1, source_target_pairs={{0,128},{1,129},{2,130},{3,131},{4,132},{5,133},{6,134},{7,135},{8... | collective-permute-start | bytes 4718600 | tf_op jit(solution)/shard_map/ppermute | solution.py:30
  35.2 107.3 %collective-permute-start = (f32[3,32,1,512]{3,2,1,0:T(1,128)}, f32[3,32,1,512]{3,2,1,0:T(1,128)}, u32[]{:S(2)}, u32[]{:S(2)}) collective-permute-start(f32[3,32,1,512]{3,2,1,0:T(1,128)} %get-tuple-element.20), channel_id=1, source_target_pairs={{1,0},{2,1},{3,2},{5,4},{6,5},{7,6},{9,8},{10,9},{11,10},{13,12},{... | collective-permute-start | bytes 589832 | tf_op jit(solution)/shard_map/ppermute | solution.py:20
  36.4 106.0 %collective-permute-start.1 = (f32[3,32,1,512]{3,2,1,0:T(1,128)}, f32[3,32,1,512]{3,2,1,0:T(1,128)}, u32[]{:S(2)}, u32[]{:S(2)}) collective-permute-start(f32[3,32,1,512]{3,2,1,0:T(1,128)} %get-tuple-element.21), channel_id=1, source_target_pairs={{0,1},{1,2},{2,3},{4,5},{5,6},{6,7},{8,9},{9,10},{10,11},{12,13},{... | collective-permute-start | bytes 589832 | tf_op jit(solution)/shard_map/ppermute | solution.py:18
  64.8 31.4 %copy-start.3 = (f32[1024,1]{1,0:T(8,128)}, f32[1024,1]{1,0:T(8,128)S(1)}, u32[]{:S(2)}) copy-start(f32[1024,1]{1,0:T(8,128)S(1)} %copy.24) | copy-start | bytes 12292
  86.3 2.7 copy-start
  102.3 8.4 %copy-start.9 = (f32[257]{0:T(512)S(1)}, f32[257]{0:T(512)}, u32[]{:S(2)}) copy-start(f32[257]{0:T(512)} %param.7) | copy-start | bytes 3088
  102.3 36.3 %all-to-all-start.1 = ((f32[3,1024,128]{2,0,1:T(4,128)}), f32[3,1024,128]{2,0,1:T(4,128)}, u32[]{:S(2)}, u32[]{:S(2)}) async-start(f32[3,1024,128]{2,0,1:T(4,128)} %copy.30), calls=%async_computation.1 | async-start | bytes 4194304 | tf_op jit(solution)/shard_map/all_to_all | solution.py:74
  118.2 4.0 %copy-start.5 = (f32[512,511]{1,0:T(8,128)}, f32[512,511]{1,0:T(8,128)S(1)}, u32[]{:S(2)}) copy-start(f32[512,511]{1,0:T(8,128)S(1)} %reshape.82) | copy-start | bytes 3139588
  125.3 1.3 copy-start.6
  160.8 29.0 %all-to-all-start.2 = ((f32[32,1,12288]{2,1,0:T(1,128)}), f32[32,1,12288]{2,1,0:T(1,128)}, u32[]{:S(2)}, u32[]{:S(2)}) async-start(f32[32,1,12288]{2,1,0:T(1,128)} %reshape.93), calls=%async_computation.2 | async-start | bytes 3145728 | tf_op jit(solution)/shard_map/all_to_all | solution.py:70
  167.5 101.1 %collective-permute-start.5 = (f32[3,32,8,512]{3,2,1,0:T(8,128)S(1)}, f32[3,32,8,512]{3,2,1,0:T(8,128)}, u32[]{:S(2)}, u32[]{:S(2)}) collective-permute-start(f32[3,32,8,512]{3,2,1,0:T(8,128)S(1)} %fusion.28), channel_id=1, source_target_pairs={{0,128},{1,129},{2,130},{3,131},{4,132},{5,133},{6,134},{7,135},{8... | collective-permute-start | bytes 4718600 | tf_op jit(solution)/shard_map/ppermute | solution.py:30
  210.6 2.7 copy-start.1
  213.2 4.9 %copy-start.4 = (f32[1024,1]{1,0:T(8,128)S(1)}, f32[1024,1]{1,0:T(8,128)}, u32[]{:S(2)}) copy-start(f32[1024,1]{1,0:T(8,128)} %copy-done.3) | copy-start | bytes 12292
  227.9 34.4 %all-to-all-start.3 = ((f32[3,1024,128]{2,0,1:T(4,128)}), f32[3,1024,128]{2,0,1:T(4,128)}, u32[]{:S(2)}, u32[]{:S(2)}) async-start(f32[3,1024,128]{2,0,1:T(4,128)} %copy.39), calls=%async_computation.3 | async-start | bytes 4194304 | tf_op jit(solution)/shard_map/all_to_all | solution.py:74
  235.4 33.2 %collective-permute-start.3 = (f32[3,32,1,512]{3,2,1,0:T(1,128)}, f32[3,32,1,512]{3,2,1,0:T(1,128)}, u32[]{:S(2)}, u32[]{:S(2)}) collective-permute-start(f32[3,32,1,512]{3,2,1,0:T(1,128)} %get-tuple-element.12), channel_id=1, source_target_pairs={{1,0},{2,1},{3,2},{5,4},{6,5},{7,6},{9,8},{10,9},{11,10},{13,12},{... | collective-permute-start | bytes 589832 | tf_op jit(solution)/shard_map/ppermute | solution.py:20
  236.6 9.9 %copy-start.7 = (f32[1,32,8,512]{3,2,1,0:T(8,128)S(1)}, f32[1,32,8,512]{3,2,1,0:T(8,128)}, u32[]{:S(2)}) copy-start(f32[1,32,8,512]{3,2,1,0:T(8,128)} %param.5) | copy-start | bytes 1572868
  236.7 31.9 %collective-permute-start.4 = (f32[3,32,1,512]{3,2,1,0:T(1,128)}, f32[3,32,1,512]{3,2,1,0:T(1,128)}, u32[]{:S(2)}, u32[]{:S(2)}) collective-permute-start(f32[3,32,1,512]{3,2,1,0:T(1,128)} %get-tuple-element.13), channel_id=1, source_target_pairs={{0,1},{1,2},{2,3},{4,5},{5,6},{6,7},{8,9},{9,10},{10,11},{12,13},{... | collective-permute-start | bytes 589832 | tf_op jit(solution)/shard_map/ppermute | solution.py:18
where the time goes:
time: 278 us; the launch traced here: 274 us
  local copies, waits for them, and re-layouts  101 us (36%)
  starting transfers between devices  55 us (20%)
  waiting for transfers between devices  45.3 us (16%)
  matrix products  43.6 us (16%)
  other arithmetic  29 us (10%)
    unnamed x29, local copies, waits for them, and re-layouts  41.7 us
    all_to_all x2, waiting for transfers between devices, tendency(): lax.all_to_all(gradient, 'gx', split_axis=1, concat_axis=2, tiled=True)  25.4 us
    dot_general x6, matrix products, tendency(): jnp.dot(table_x, pencils[comp], precision=lax.Precision.HIGHEST)  21.7 us
    all_to_all x2, waiting for transfers between devices, tendency(): lax.all_to_all(flat_block, 'gx', split_axis=2, concat_axis=1, tiled=True)  19.8 us
    all_to_all x2, starting transfers between devices, tendency(): lax.all_to_all(flat_block, 'gx', split_axis=2, concat_axis=1, tiled=True)  15.4 us
    all_to_all x2, starting transfers between devices, tendency(): lax.all_to_all(gradient, 'gx', split_axis=1, concat_axis=2, tiled=True)  14.8 us
    all_to_all x2, other arithmetic, tendency(): lax.all_to_all(flat_block, 'gx', split_axis=2, concat_axis=1, tiled=True)  13.7 us
    all_to_all x3, local copies, waits for them, and re-layouts, tendency(): lax.all_to_all(flat_block, 'gx', split_axis=2, concat_axis=1, tiled=True)  13.1 us
  transfers between devices with their start and end apart: 10, of which 3 were waited for; matrix products, arithmetic and copies ran while one was open for 48% of the time, Pallas kernels for 0%

commit v1 on v0

v1 whole, which is shorter than its diff:
```python
import functools

import jax
import jax.numpy as jnp
import ml_dtypes
import numpy as np
from jax import lax
from jax.experimental import pallas as pl
from jax.experimental.pallas import tpu as pltpu
from jax.sharding import PartitionSpec as P

MESH = pl.DeviceIdType.MESH
ANY = pl.ANY
F32 = jnp.float32
BF16 = jnp.bfloat16
fringe_peak = 4.0
dt = 0.05
LANES = 128


def halves(x):
    high = x.astype(np.float32).astype(ml_dtypes.bfloat16)
    low = (x - high.astype(np.float64)).astype(ml_dtypes.bfloat16)
    return high, low


def transform_tables(half):
    points = np.arange(half, dtype=np.int64)
    forward, inverse = [], []
    for odd in range(2):
        modes = 2 * np.arange(half // 2, dtype=np.int64) + odd
        angle = 2.0 * np.pi * (np.outer(modes, points) % (2 * half)) / (2 * half)
        forward.append(np.concatenate([np.cos(angle), np.sin(angle)], 0))
        inverse.append(np.concatenate([-np.sin(angle), np.cos(angle)], 0).T)
    return np.stack(forward), np.stack(inverse)


def mode_weights(stream_gain, span_gain, total_x, width_y):
    wave_y = (-(2.0 / width_y) * 2.0 * np.pi / width_y) * np.arange(width_y // 2)
    wave_x = ((2.0 / total_x) * 2.0 * np.pi / total_x) * np.arange(total_x // 2)
    along_y = span_gain[: width_y // 2] * wave_y.astype(np.float32)
    along_x = (stream_gain[: total_x // 2] * wave_x.astype(np.float32)).reshape(-1, 2)
    rows = jnp.stack([along_y, along_x[:, 0], along_x[:, 1]])
    return jnp.concatenate([rows, rows], 1)


def split(x):
    high = x.astype(BF16)
    return high, (x - high.astype(F32)).astype(BF16)


def dot(a, b):
    return jnp.dot(a, b, preferred_element_type=F32)


def step_kernel(
    groups, sheets, v_hbm, drag_hbm, weights, forward_hbm, inverse_hbm, lam_hbm, out_hbm,
    v_raw, drag_raw, out_raw, forward, inverse, lam, table,
    v_here, f_here, drag, h_here, g_here, partial, stack, span_grad,
    v_pen, h_pen, f_pen, g_pen, rest, up_v, up_f,
    load_sem, own_sem, send_sem, recv_sem, halo_send, halo_recv, up_send, up_recv,
):
    me, gz, sec = lax.axis_index("gx"), lax.axis_index("gz"), lax.axis_index("sec")
    levels, cells, width = drag.shape
    half = table.shape[-1]
    total = 2 * half
    bands = width // LANES
    fringe = total - total // 4
    shape_y, shape_x = 4, groups // 8

    def peer(k):
        y, x, core = me // (2 * shape_x), (me // 2) % shape_x, me % 2
        y = (y + k // (2 * shape_x)) % shape_y
        x = (x + (k // 2) % shape_x) % shape_x
        return (y * shape_x + x) * 2 + (core + k) % 2

    def rows_of(device):
        return pl.ds(pl.multiple_of(device * cells, cells), cells)

    def band_of(device):
        return pl.ds(pl.multiple_of((device % bands) * LANES, LANES), LANES)

    def wait(ref, sem):
        pltpu.make_async_copy(ref, ref, sem).wait()

    def remote(source, target, sent, arrived, where):
        pltpu.make_async_remote_copy(
            source, target, sent, arrived, device_id=where, device_id_type=MESH
        ).start()

    def to_pencils(source, base, target, comps, slot):
        def block(p):
            return source.at[comps, base + p // bands, :, band_of(p)]

        def body(k, carry):
            p = peer(k)
            remote(block(p), target.at[comps, rows_of(me)], send_sem.at[slot], recv_sem.at[slot], {"gx": p})
            return carry

        lax.fori_loop(1, groups, body, 0)
        pltpu.make_async_copy(block(me), target.at[comps, rows_of(me)], recv_sem.at[slot]).start()

    def to_blocks(source, target, base, comp, slot):
        place = target.at[comp, base + me // bands, :, band_of(me)]

        def body(k, carry):
            p = peer(k)
            remote(source.at[comp, rows_of(p)], place, send_sem.at[slot], recv_sem.at[slot], {"gx": p})
            return carry

        lax.fori_loop(1, groups, body, 0)
        pltpu.make_async_copy(source.at[comp, rows_of(me)], place, recv_sem.at[slot]).start()

    def send_halo(fields, slot):
        @pl.when(gz > 0)
        def _():
            remote(fields.at[:, 1], fields.at[:, levels + 1], halo_send.at[slot, 0], halo_recv.at[slot, 0], {"gz": gz - 1})

        @pl.when(gz < sheets - 1)
        def _():
            remote(fields.at[:, levels], fields.at[:, 0], halo_send.at[slot, 1], halo_recv.at[slot, 1], {"gz": gz + 1})

    def wait_halo(fields, slot):
        @pl.when(gz > 0)
        def _():
            wait(fields.at[:, 0], halo_recv.at[slot, 1])

        @pl.when(gz < sheets - 1)
        def _():
            wait(fields.at[:, levels + 1], halo_recv.at[slot, 0])

    def wait_halo_sent(fields, slot):
        @pl.when(gz > 0)
        def _():
            wait(fields.at[:, 1], halo_send.at[slot, 0])

        @pl.when(gz < sheets - 1)
        def _():
            wait(fields.at[:, levels], halo_send.at[slot, 1])

    loads = [pltpu.make_async_copy(v_hbm.at[c], v_raw.at[c], load_sem.at[c]) for c in range(3)]
    loads += [
        pltpu.make_async_copy(inverse_hbm, inverse, load_sem.at[3]),
        pltpu.make_async_copy(forward_hbm, forward, load_sem.at[4]),
        pltpu.make_async_copy(drag_hbm, drag_raw, load_sem.at[5]),
        pltpu.make_async_copy(lam_hbm, lam, load_sem.at[6]),
    ]
    for load in loads:
        load.start()
    barrier = pltpu.get_barrier_semaphore()

    def greet(k, carry):
        pl.semaphore_signal(barrier, inc=1, device_id={"gx": peer(k)}, device_id_type=MESH)
        return carry

    lax.fori_loop(1, groups, greet, 0)
    pl.semaphore_signal(barrier, inc=1, device_id={"sec": 1 - sec}, device_id_type=MESH)

    @pl.when(gz > 0)
    def _():
        pl.semaphore_signal(barrier, inc=1, device_id={"gz": gz - 1}, device_id_type=MESH)

    @pl.when(gz < sheets - 1)
    def _():
        pl.semaphore_signal(barrier, inc=1, device_id={"gz": gz + 1}, device_id_type=MESH)

    for c in range(3):
        loads[c].wait()
        for z in range(levels):
            v_here[c, 1 + z] = v_raw[c, :, z, :]

    @pl.when((gz == 0) | (gz == sheets - 1))
    def _():
        pl.semaphore_wait(barrier, groups + 1)

    @pl.when((gz > 0) & (gz < sheets - 1))
    def _():
        pl.semaphore_wait(barrier, groups + 2)

    send_halo(v_here, 0)
    to_pencils(v_here, 1, v_pen, slice(None), 0)

    @pl.when(gz == 0)
    def _():
        v_here[:, 0] = jnp.zeros((3, cells, width), F32)
        f_here[:, 0] = jnp.zeros((3, cells, width), F32)

    @pl.when(gz == sheets - 1)
    def _():
        v_here[:, levels + 1] = jnp.zeros((3, cells, width), F32)
        f_here[:, levels + 1] = jnp.zeros((3, cells, width), F32)

    loads[3].wait()
    loads[4].wait()

    def build(j, carry):
        kind = j // 2
        scaled_high, scaled_low = split(inverse[kind] * weights[pl.ds(j, 1), :])
        matrix = dot(scaled_high, forward[kind, 0]) + (
            dot(scaled_low, forward[kind, 0]) + dot(scaled_high, forward[kind, 1])
        )
        table[j, 0], table[j, 1] = split(matrix)
        return carry

    lax.fori_loop(0, 3, build, 0)
    loads[5].wait()
    for z in range(levels):
        drag[z] = drag_raw[:, z, :]

    def local_terms(fields, comp, put):
        def spread(z, carry):
            at = pl.ds(pl.multiple_of(z * cells, cells), cells)
            low_at = pl.ds(pl.multiple_of((levels + z) * cells, cells), cells)
            stack[at], stack[low_at] = split(fields[comp, 1 + z])
            return carry

        lax.fori_loop(0, levels, spread, 0)
        rows = levels * cells
        both = dot(stack[...], table[0, 0])
        span_grad[...] = (both[:rows] + both[rows:]) + dot(stack[:rows], table[0, 1])

        def level(z, carry):
            at = pl.ds(pl.multiple_of(z * cells, cells), cells)
            rise = 0.5 * (fields[comp, 2 + z] - fields[comp, z])
            here = fields[comp, 1 + z]
            advect = fields[1, 1 + z] * span_grad[at] + fields[2, 1 + z] * rise
            put(z, here, -advect - drag[z] * jnp.abs(fields[0, 1 + z]) * here)
            return carry

        lax.fori_loop(0, levels, level, 0)

    def stream_grad(fields, comp):
        near, far = fields[comp, :half], fields[comp, half:]
        parts = []
        for j, mixed in ((1, near + far), (2, near - far)):
            high, low = split(mixed)
            both = dot(table[j, 0], jnp.concatenate([high, low], 1))
            parts.append((both[:, :LANES] + both[:, LANES:]) + dot(table[j, 1], high))
        return parts[0] + parts[1], parts[0] - parts[1]

    wait_halo(v_here, 0)
    for c in range(3):

        def keep(z, here, value, c=c):
            h_here[c, z] = value

        local_terms(v_here, c, keep)
        to_pencils(h_here, 0, h_pen, c, 1 + c)

    loads[6].wait()
    wait(v_pen, recv_sem.at[0])
    lift = pl.ds(fringe, total - fringe)

    @pl.when(sec == 0)
    def _():
        remote(v_pen.at[:, lift], up_v, up_send.at[0], up_recv.at[0], {"sec": 1})

    for c in range(3):
        near, far = stream_grad(v_pen, c)
        rest[c, :half] = v_pen[c, :half] - dt * (v_pen[0, :half] * near)
        rest[c, half:] = v_pen[c, half:] - dt * (v_pen[0, half:] * far)

    @pl.when(sec == 1)
    def _():
        wait(up_v, up_recv.at[0])
        for c in range(3):
            rest[c, lift] += dt * (lam[...] * (up_v[c] - v_pen[c, lift]))

    for c in range(3):
        wait(h_pen.at[c], recv_sem.at[1 + c])
        f_pen[c] = rest[c] + dt * h_pen[c]
        to_blocks(f_pen, f_here, 1, c, 4 + c)

        @pl.when(sec == 0)
        def _(c=c):
            remote(f_pen.at[c, lift], up_f.at[c], up_send.at[1 + c], up_recv.at[1 + c], {"sec": 1})

    for c in range(3):
        near, far = stream_grad(f_pen, c)
        g_pen[c, :half] = -f_pen[0, :half] * near
        g_pen[c, half:] = -f_pen[0, half:] * far

        @pl.when(sec == 1)
        def _(c=c):
            wait(up_f.at[c], up_recv.at[1 + c])
            g_pen[c, lift] += lam[...] * (up_f[c] - f_pen[c, lift])

        to_blocks(g_pen, g_here, 0, c, 7 + c)

    for c in range(3):
        wait(g_here.at[c], recv_sem.at[4 + c])
    send_halo(f_here, 1)
    wait_halo(f_here, 1)
    for c in range(3):

        def keep(z, here, value, c=c):
            partial[c, z] = 0.5 * v_here[c, 1 + z] + 0.5 * (here + dt * value)

        local_terms(f_here, c, keep)

    stores = []
    for c in range(3):
        wait(g_here.at[c], recv_sem.at[7 + c])
        for z in range(levels):
            out_raw[c, :, z, :] = partial[c, z] + (0.5 * dt) * g_here[c, z]
        store = pltpu.make_async_copy(out_raw.at[c], out_hbm.at[c], own_sem.at[c])
        store.start()
        stores.append(store)

    others = pl.ds(0, total - cells)
    wait(v_pen.at[:, others], send_sem.at[0])
    for slot in range(1, 10):
        wait(v_pen.at[0, others], send_sem.at[slot])
    wait_halo_sent(v_here, 0)
    wait_halo_sent(f_here, 1)

    @pl.when(sec == 0)
    def _():
        wait(up_v, up_send.at[0])
        for c in range(3):
            wait(up_f.at[c], up_send.at[1 + c])

    for store in stores:
        store.wait()


def solution(mesh):
    groups, sheets = mesh.shape["gx"], mesh.shape["gz"]

    def shards(velocity, drag, stream_gain, span_gain):
        fields, drag_here = velocity[0], drag[0]
        _, cells, levels, width = fields.shape
        total = cells * groups
        half = total // 2
        pencil = (3, total, LANES)
        block = (3, levels, cells, width)
        padded = (3, levels + 2, cells, width)
        fringe = total // 4
        forward, inverse = transform_tables(half)
        high, low = halves(forward)
        forward = np.stack([high, low], 1)
        phases = np.pi * (np.arange(fringe) + 0.5) / fringe
        lam = np.repeat((fringe_peak * np.sin(phases) ** 2)[:, None], LANES, 1)
        weights = mode_weights(stream_gain, span_gain, total, width)
        dma = pltpu.SemaphoreType.DMA
        flops = 2 * 3 * (2 * total * half * LANES * 4 + 2 * half * half * half * 3)
        out = pl.pallas_call(
            functools.partial(step_kernel, groups, sheets),
            name="fringe_step",
            out_shape=jax.ShapeDtypeStruct(fields.shape, F32),
            in_specs=[pl.BlockSpec(memory_space=ANY)] * 2
            + [pl.BlockSpec(memory_space=pltpu.VMEM)]
            + [pl.BlockSpec(memory_space=ANY)] * 3,
            out_specs=pl.BlockSpec(memory_space=ANY),
            scratch_shapes=[
                pltpu.VMEM(fields.shape, F32),
                pltpu.VMEM(drag_here.shape, F32),
                pltpu.VMEM(fields.shape, F32),
                pltpu.VMEM((2, 2, half, half), BF16),
                pltpu.VMEM((2, half, half), F32),
                pltpu.VMEM((fringe, LANES), F32),
                pltpu.VMEM((3, 2, half, half), BF16),
                pltpu.VMEM(padded, F32),
                pltpu.VMEM(padded, F32),
                pltpu.VMEM((levels, cells, width), F32),
                pltpu.VMEM(block, F32),
                pltpu.VMEM(block, F32),
                pltpu.VMEM(block, F32),
                pltpu.VMEM((2 * levels * cells, width), BF16),
                pltpu.VMEM((levels * cells, width), F32),
                pltpu.VMEM(pencil, F32),
                pltpu.VMEM(pencil, F32),
                pltpu.VMEM(pencil, F32),
                pltpu.VMEM(pencil, F32),
                pltpu.VMEM(pencil, F32),
                pltpu.VMEM((3, fringe, LANES), F32),
                pltpu.VMEM((3, fringe, LANES), F32),
                dma((7,)),
                dma((3,)),
                dma((10,)),
                dma((10,)),
                dma((2, 2)),
                dma((2, 2)),
                dma((4,)),
                dma((4,)),
            ],
            compiler_params=pltpu.CompilerParams(
                collective_id=0, has_side_effects=True, vmem_limit_bytes=56 * 2**20
            ),
            cost_estimate=pl.CostEstimate(flops=flops, bytes_accessed=10**7, transcendentals=0),
        )(fields, drag_here, weights, forward, inverse.astype(np.float32), lam.astype(np.float32))
        return out[None]

    return jax.shard_map(
        shards,
        mesh=mesh,
        in_specs=(P("sec", None, "gx", "gz", None), P("sec", "gx", "gz", None), P(), P()),
        out_specs=P("sec", None, "gx", "gz", None),
        check_vma=False,
    )
```

time: 278 us -> 104 us (0.37)
  the two profiles are of different devices: /device:TPU:1 before, /device:TPU:193 now
where the time goes in v1:
time: 104 us
  Pallas kernels  98.5 us (95%)
  local copies, waits for them, and re-layouts  3.01 us (3%)
  other arithmetic  2.02 us (2%)
    pallas_call x1, Pallas kernels, shards(): pl.pallas_call(functools.partial(step_kernel, groups, sheets), name='frin...  98.5 us
    unnamed x1, local copies, waits for them, and re-layouts  2.67 us

profile of v1, /device:TPU:193, one launch (start us, length us, event | category | flops | bytes accessed | tf_op | source)
XLA Modules:
  0.0 103.6 jit_solution(17071772442795189069)
XLA Ops:
  0.0 0.7 slice_multiply_fusion.1
  0.7 0.7 slice_multiply_fusion
  1.4 0.1 reshape.3
  1.6 0.2 slice_reduce_fusion.1
  1.8 0.6 maximum_maximum_fusion.weights
  2.4 98.5 %fringe_step.1 = f32[3,32,8,512]{3,2,1,0:T(8,128)} custom-call(f32[3,32,8,512]{3,2,1,0:T(8,128)} %bitcast.10, f32[32,8,512]{2,1,0:T(8,128)} %bitcast.11, f32[3,512]{1,0:T(4,128)} %maximum_maximum_fusion.weights, bf16[2,2,512,512]{3,2,1,0:T(8,128)(2,1)} %constant.12.clone.forward_hbm, f32[2,512,512]{2,1,0:T(8,128)} %constant.13.clone.inverse_hbm, ...), custom_call_target="tpu_custom_call" | custom-call | flops 8053063680 | bytes 10000000 | tf_op jit(solution)/shard_map/fringe_step/pallas_call | solution.py:347
  100.9 2.7 %copy.11 = f32[1,3,32,8,512]{4,3,2,1,0:T(8,128)} copy(f32[1,3,32,8,512]{4,3,2,1,0:T(8,128)} %bitcast.6) | data formatting | bytes 3145728

commit v2 on v1

--- a/solution.py
+++ b/solution.py
@@ -66,13 +66,18 @@
     total = 2 * half
     bands = width // LANES
     fringe = total - total // 4
+    lift = pl.ds(fringe, total - fringe)
     shape_y, shape_x = 4, groups // 8
 
-    def peer(k):
-        y, x, core = me // (2 * shape_x), (me // 2) % shape_x, me % 2
-        y = (y + k // (2 * shape_x)) % shape_y
-        x = (x + (k // 2) % shape_x) % shape_x
-        return (y * shape_x + x) * 2 + (core + k) % 2
+    far_first = sorted(
+        [(y, x, core) for y in range(shape_y) for x in range(shape_x) for core in range(2)][1:],
+        key=lambda o: -(min(o[0], shape_y - o[0]) + min(o[1], shape_x - o[1])),
+    )
+
+    def peer(offset):
+        y = (me // (2 * shape_x) + offset[0]) % shape_y
+        x = (me // 2 + offset[1]) % shape_x
+        return (y * shape_x + x) * 2 + (me + offset[2]) % 2
 
     def rows_of(device):
         return pl.ds(pl.multiple_of(device * cells, cells), cells)
@@ -88,27 +93,21 @@
             source, target, sent, arrived, device_id=where, device_id_type=MESH
         ).start()
 
-    def to_pencils(source, base, target, comps, slot):
+    def to_pencils(source, base, target, comp, slot):
         def block(p):
-            return source.at[comps, base + p // bands, :, band_of(p)]
-
-        def body(k, carry):
-            p = peer(k)
-            remote(block(p), target.at[comps, rows_of(me)], send_sem.at[slot], recv_sem.at[slot], {"gx": p})
-            return carry
-
-        lax.fori_loop(1, groups, body, 0)
-        pltpu.make_async_copy(block(me), target.at[comps, rows_of(me)], recv_sem.at[slot]).start()
+            return source.at[comp, base + p // bands, :, band_of(p)]
+
+        for offset in far_first:
+            p = peer(offset)
+            remote(block(p), target.at[comp, rows_of(me)], send_sem.at[slot], recv_sem.at[slot], {"gx": p})
+        pltpu.make_async_copy(block(me), target.at[comp, rows_of(me)], recv_sem.at[slot]).start()
 
     def to_blocks(source, target, base, comp, slot):
         place = target.at[comp, base + me // bands, :, band_of(me)]
 
-        def body(k, carry):
-            p = peer(k)
+        for offset in far_first:
+            p = peer(offset)
             remote(source.at[comp, rows_of(p)], place, send_sem.at[slot], recv_sem.at[slot], {"gx": p})
-            return carry
-
-        lax.fori_loop(1, groups, body, 0)
         pltpu.make_async_copy(source.at[comp, rows_of(me)], place, recv_sem.at[slot]).start()
 
     def send_halo(fields, slot):
@@ -150,7 +149,7 @@
     barrier = pltpu.get_barrier_semaphore()
 
     def greet(k, carry):
-        pl.semaphore_signal(barrier, inc=1, device_id={"gx": peer(k)}, device_id_type=MESH)
+        pl.semaphore_signal(barrier, inc=1, device_id={"gx": (me + k) % groups}, device_id_type=MESH)
         return carry
 
     lax.fori_loop(1, groups, greet, 0)
@@ -178,7 +177,8 @@
         pl.semaphore_wait(barrier, groups + 2)
 
     send_halo(v_here, 0)
-    to_pencils(v_here, 1, v_pen, slice(None), 0)
+    for c in range(3):
+        to_pencils(v_here, 1, v_pen, c, c)
 
     @pl.when(gz == 0)
     def _():
@@ -245,16 +245,15 @@
             h_here[c, z] = value
 
         local_terms(v_here, c, keep)
-        to_pencils(h_here, 0, h_pen, c, 1 + c)
+        wait(v_pen.at[c], recv_sem.at[c])
+
+        @pl.when(sec == 0)
+        def _(c=c):
+            remote(v_pen.at[c, lift], up_v.at[c], up_send.at[c], up_recv.at[c], {"sec": 1})
+
+        to_pencils(h_here, 0, h_pen, c, 3 + c)
 
     loads[6].wait()
-    wait(v_pen, recv_sem.at[0])
-    lift = pl.ds(fringe, total - fringe)
-
-    @pl.when(sec == 0)
-    def _():
-        remote(v_pen.at[:, lift], up_v, up_send.at[0], up_recv.at[0], {"sec": 1})
-
     for c in range(3):
         near, far = stream_grad(v_pen, c)
         rest[c, :half] = v_pen[c, :half] - dt * (v_pen[0, :half] * near)
@@ -262,18 +261,19 @@
 
     @pl.when(sec == 1)
     def _():
-        wait(up_v, up_recv.at[0])
         for c in range(3):
+            wait(up_v.at[c], up_recv.at[c])
             rest[c, lift] += dt * (lam[...] * (up_v[c] - v_pen[c, lift]))
 
     for c in range(3):
-        wait(h_pen.at[c], recv_sem.at[1 + c])
+        wait(h_pen.at[c], recv_sem.at[3 + c])
         f_pen[c] = rest[c] + dt * h_pen[c]
-        to_blocks(f_pen, f_here, 1, c, 4 + c)
 
         @pl.when(sec == 0)
         def _(c=c):
-            remote(f_pen.at[c, lift], up_f.at[c], up_send.at[1 + c], up_recv.at[1 + c], {"sec": 1})
+            remote(f_pen.at[c, lift], up_f.at[c], up_send.at[3 + c], up_recv.at[3 + c], {"sec": 1})
+
+        to_blocks(f_pen, f_here, 1, c, 6 + c)
 
     for c in range(3):
         near, far = stream_grad(f_pen, c)
@@ -282,13 +282,13 @@
 
         @pl.when(sec == 1)
         def _(c=c):
-            wait(up_f.at[c], up_recv.at[1 + c])
+            wait(up_f.at[c], up_recv.at[3 + c])
             g_pen[c, lift] += lam[...] * (up_f[c] - f_pen[c, lift])
 
-        to_blocks(g_pen, g_here, 0, c, 7 + c)
-
-    for c in range(3):
-        wait(g_here.at[c], recv_sem.at[4 + c])
+        to_blocks(g_pen, g_here, 0, c, 9 + c)
+
+    for c in range(3):
+        wait(g_here.at[c], recv_sem.at[6 + c])
     send_halo(f_here, 1)
     wait_halo(f_here, 1)
     for c in range(3):
@@ -300,7 +300,7 @@
 
     stores = []
     for c in range(3):
-        wait(g_here.at[c], recv_sem.at[7 + c])
+        wait(g_here.at[c], recv_sem.at[9 + c])
         for z in range(levels):
             out_raw[c, :, z, :] = partial[c, z] + (0.5 * dt) * g_here[c, z]
         store = pltpu.make_async_copy(out_raw.at[c], out_hbm.at[c], own_sem.at[c])
@@ -308,17 +308,16 @@
         stores.append(store)
 
     others = pl.ds(0, total - cells)
-    wait(v_pen.at[:, others], send_sem.at[0])
-    for slot in range(1, 10):
+    for slot in range(12):
         wait(v_pen.at[0, others], send_sem.at[slot])
     wait_halo_sent(v_here, 0)
     wait_halo_sent(f_here, 1)
 
     @pl.when(sec == 0)
     def _():
-        wait(up_v, up_send.at[0])
         for c in range(3):
-            wait(up_f.at[c], up_send.at[1 + c])
+            wait(up_v.at[c], up_send.at[c])
+            wait(up_f.at[c], up_send.at[3 + c])
 
     for store in stores:
         store.wait()
@@ -377,12 +376,12 @@
                 pltpu.VMEM((3, fringe, LANES), F32),
                 dma((7,)),
                 dma((3,)),
-                dma((10,)),
-                dma((10,)),
+                dma((12,)),
+                dma((12,)),
                 dma((2, 2)),
                 dma((2, 2)),
-                dma((4,)),
-                dma((4,)),
+                dma((6,)),
+                dma((6,)),
             ],
             compiler_params=pltpu.CompilerParams(
                 collective_id=0, has_side_effects=True, vmem_limit_bytes=56 * 2**20

time: 104 us -> 87.6 us (0.84)
  the two profiles are of different devices: /device:TPU:193 before, /device:TPU:1 now
where the time goes in v2:
time: 87.6 us; the launch traced here: 87.4 us
  Pallas kernels  82.4 us (94%)
  local copies, waits for them, and re-layouts  3.01 us (3%)
  other arithmetic  2.02 us (2%)
    pallas_call x1, Pallas kernels, shards(): pl.pallas_call(functools.partial(step_kernel, groups, sheets), name='frin...  82.4 us
    unnamed x1, local copies, waits for them, and re-layouts  2.67 us

profile of v2, /device:TPU:1, one launch (start us, length us, event | category | flops | bytes accessed | tf_op | source)
XLA Modules:
  0.0 87.4 jit_solution(9514296159481894048)
XLA Ops:
  0.0 0.7 slice_multiply_fusion.1
  0.7 0.7 slice_multiply_fusion
  1.4 0.1 reshape.3
  1.6 0.2 slice_reduce_fusion.1
  1.8 0.6 maximum_maximum_fusion.weights
  2.4 82.4 %fringe_step.1 = f32[3,32,8,512]{3,2,1,0:T(8,128)} custom-call(f32[3,32,8,512]{3,2,1,0:T(8,128)} %bitcast.10, f32[32,8,512]{2,1,0:T(8,128)} %bitcast.11, f32[3,512]{1,0:T(4,128)} %maximum_maximum_fusion.weights, bf16[2,2,512,512]{3,2,1,0:T(8,128)(2,1)} %constant.12.clone.forward_hbm, f32[2,512,512]{2,1,0:T(8,128)} %constant.13.clone.inverse_hbm, ...), custom_call_target="tpu_custom_call" | custom-call | flops 8053063680 | bytes 10000000 | tf_op jit(solution)/shard_map/fringe_step/pallas_call | solution.py:346
  84.7 2.7 %copy.11 = f32[1,3,32,8,512]{4,3,2,1,0:T(8,128)} copy(f32[1,3,32,8,512]{4,3,2,1,0:T(8,128)} %bitcast.6) | data formatting | bytes 3145728

commit v3 on v2

--- a/solution.py
+++ b/solution.py
@@ -35,13 +35,16 @@
     return np.stack(forward), np.stack(inverse)
 
 
-def mode_weights(stream_gain, span_gain, total_x, width_y):
-    wave_y = (-(2.0 / width_y) * 2.0 * np.pi / width_y) * np.arange(width_y // 2)
-    wave_x = ((2.0 / total_x) * 2.0 * np.pi / total_x) * np.arange(total_x // 2)
-    along_y = span_gain[: width_y // 2] * wave_y.astype(np.float32)
-    along_x = (stream_gain[: total_x // 2] * wave_x.astype(np.float32)).reshape(-1, 2)
-    rows = jnp.stack([along_y, along_x[:, 0], along_x[:, 1]])
-    return jnp.concatenate([rows, rows], 1)
+def wave_numbers(total_x, width_y):
+    rows = np.zeros((2, total_x // 2))
+    rows[0, : width_y // 2] = -(2.0 / width_y) * 2.0 * np.pi / width_y * np.arange(width_y // 2)
+    rows[1] = (2.0 / total_x) * 2.0 * np.pi / total_x * np.arange(total_x // 2)
+    return rows.astype(np.float32)
+
+
+def even_then_odd(half):
+    order = np.concatenate([np.arange(0, half, 2), np.arange(1, half, 2)])
+    return (np.arange(half)[:, None] == order[None]).astype(ml_dtypes.bfloat16)
 
 
 def split(x):
@@ -54,11 +57,11 @@
 
 
 def step_kernel(
-    groups, sheets, v_hbm, drag_hbm, weights, forward_hbm, inverse_hbm, lam_hbm, out_hbm,
-    v_raw, drag_raw, out_raw, forward, inverse, lam, table,
+    groups, sheets, v_hbm, drag_hbm, stream_hbm, span_hbm, wave_hbm, pick_hbm, forward_hbm, inverse_hbm, lam_hbm, out_raw,
+    v_raw, drag_raw, stream_gain, span_gain, wave, pick, weights, forward, inverse, lam, table,
     v_here, f_here, drag, h_here, g_here, partial, stack, span_grad,
     v_pen, h_pen, f_pen, g_pen, rest, up_v, up_f,
-    load_sem, own_sem, send_sem, recv_sem, halo_send, halo_recv, up_send, up_recv,
+    load_sem, send_sem, recv_sem, halo_send, halo_recv, up_send, up_recv, ready,
 ):
     me, gz, sec = lax.axis_index("gx"), lax.axis_index("gz"), lax.axis_index("sec")
     levels, cells, width = drag.shape
@@ -143,6 +146,10 @@
         pltpu.make_async_copy(forward_hbm, forward, load_sem.at[4]),
         pltpu.make_async_copy(drag_hbm, drag_raw, load_sem.at[5]),
         pltpu.make_async_copy(lam_hbm, lam, load_sem.at[6]),
+        pltpu.make_async_copy(stream_hbm, stream_gain, load_sem.at[7]),
+        pltpu.make_async_copy(span_hbm, span_gain, load_sem.at[8]),
+        pltpu.make_async_copy(wave_hbm, wave, load_sem.at[9]),
+        pltpu.make_async_copy(pick_hbm, pick, load_sem.at[10]),
     ]
     for load in loads:
         load.start()
@@ -153,11 +160,9 @@
         return carry
 
     lax.fori_loop(1, groups, greet, 0)
-    pl.semaphore_signal(barrier, inc=1, device_id={"sec": 1 - sec}, device_id_type=MESH)
-
-    @pl.when(gz > 0)
-    def _():
-        pl.semaphore_signal(barrier, inc=1, device_id={"gz": gz - 1}, device_id_type=MESH)
+    @pl.when(sec == 0)
+    def _():
+        pl.semaphore_signal(barrier, inc=1, device_id={"sec": 1}, device_id_type=MESH)
 
     @pl.when(gz < sheets - 1)
     def _():
@@ -167,18 +172,24 @@
         loads[c].wait()
         for z in range(levels):
             v_here[c, 1 + z] = v_raw[c, :, z, :]
-
-    @pl.when((gz == 0) | (gz == sheets - 1))
-    def _():
-        pl.semaphore_wait(barrier, groups + 1)
-
-    @pl.when((gz > 0) & (gz < sheets - 1))
-    def _():
-        pl.semaphore_wait(barrier, groups + 2)
+        if c == 0:
+            pl.semaphore_wait(barrier, groups - 1 + jnp.minimum(gz, 1) + sec)
+        to_pencils(v_here, 1, v_pen, c, c)
+        if c == 0:
+
+            @pl.when(gz > 0)
+            def _():
+                pl.semaphore_signal(ready.at[0], inc=1, device_id={"gz": gz - 1}, device_id_type=MESH)
+
+            @pl.when(sec == 1)
+            def _():
+                pl.semaphore_signal(ready.at[1], inc=1, device_id={"sec": 0}, device_id_type=MESH)
+
+    @pl.when(gz < sheets - 1)
+    def _():
+        pl.semaphore_wait(ready.at[0], 1)
 
     send_halo(v_here, 0)
-    for c in range(3):
-        to_pencils(v_here, 1, v_pen, c, c)
 
     @pl.when(gz == 0)
     def _():
@@ -190,6 +201,19 @@
         v_here[:, levels + 1] = jnp.zeros((3, cells, width), F32)
         f_here[:, levels + 1] = jnp.zeros((3, cells, width), F32)
 
+    for load in loads[7:]:
+        load.wait()
+    quarter = half // 2
+    along_y = span_gain[pl.ds(0, quarter)].reshape(1, quarter) * wave[0:1, :quarter]
+    along_x = stream_gain[pl.ds(0, half)].reshape(1, half) * wave[1:2]
+    sorted_x, left = jnp.zeros((16, half), F32), jnp.broadcast_to(along_x, (16, half))
+    for _ in range(3):
+        part = left.astype(BF16)
+        sorted_x = sorted_x + dot(part, pick[...])
+        left = left - part.astype(F32)
+    weights[0:1, :] = jnp.concatenate([along_y, along_y], 1)
+    weights[1:2, :] = jnp.concatenate([sorted_x[0:1, :quarter]] * 2, 1)
+    weights[2:3, :] = jnp.concatenate([sorted_x[0:1, quarter:]] * 2, 1)
     loads[3].wait()
     loads[4].wait()
 
@@ -249,6 +273,8 @@
 
         @pl.when(sec == 0)
         def _(c=c):
+            if c == 0:
+                pl.semaphore_wait(ready.at[1], 1)
             remote(v_pen.at[c, lift], up_v.at[c], up_send.at[c], up_recv.at[c], {"sec": 1})
 
         to_pencils(h_here, 0, h_pen, c, 3 + c)
@@ -298,14 +324,10 @@
 
         local_terms(f_here, c, keep)
 
-    stores = []
     for c in range(3):
         wait(g_here.at[c], recv_sem.at[9 + c])
         for z in range(levels):
             out_raw[c, :, z, :] = partial[c, z] + (0.5 * dt) * g_here[c, z]
-        store = pltpu.make_async_copy(out_raw.at[c], out_hbm.at[c], own_sem.at[c])
-        store.start()
-        stores.append(store)
 
     others = pl.ds(0, total - cells)
     for slot in range(12):
@@ -318,9 +340,6 @@
         for c in range(3):
             wait(up_v.at[c], up_send.at[c])
             wait(up_f.at[c], up_send.at[3 + c])
-
-    for store in stores:
-        store.wait()
 
 
 def solution(mesh):
@@ -340,21 +359,23 @@
         forward = np.stack([high, low], 1)
         phases = np.pi * (np.arange(fringe) + 0.5) / fringe
         lam = np.repeat((fringe_peak * np.sin(phases) ** 2)[:, None], LANES, 1)
-        weights = mode_weights(stream_gain, span_gain, total, width)
+        wave, pick = wave_numbers(total, width), even_then_odd(half)
         dma = pltpu.SemaphoreType.DMA
         flops = 2 * 3 * (2 * total * half * LANES * 4 + 2 * half * half * half * 3)
         out = pl.pallas_call(
             functools.partial(step_kernel, groups, sheets),
             name="fringe_step",
-            out_shape=jax.ShapeDtypeStruct(fields.shape, F32),
-            in_specs=[pl.BlockSpec(memory_space=ANY)] * 2
-            + [pl.BlockSpec(memory_space=pltpu.VMEM)]
-            + [pl.BlockSpec(memory_space=ANY)] * 3,
-            out_specs=pl.BlockSpec(memory_space=ANY),
+            out_shape=pltpu.VMEM(fields.shape, F32),
+            in_specs=[pl.BlockSpec(memory_space=ANY)] * 9,
+            out_specs=pl.BlockSpec(memory_space=pltpu.VMEM),
             scratch_shapes=[
                 pltpu.VMEM(fields.shape, F32),
                 pltpu.VMEM(drag_here.shape, F32),
-                pltpu.VMEM(fields.shape, F32),
+                pltpu.VMEM(stream_gain.shape, F32),
+                pltpu.VMEM(span_gain.shape, F32),
+                pltpu.VMEM((2, half), F32),
+                pltpu.VMEM((half, half), BF16),
+                pltpu.VMEM((8, half), F32),
                 pltpu.VMEM((2, 2, half, half), BF16),
                 pltpu.VMEM((2, half, half), F32),
                 pltpu.VMEM((fringe, LANES), F32),
@@ -374,20 +395,23 @@
                 pltpu.VMEM(pencil, F32),
                 pltpu.VMEM((3, fringe, LANES), F32),
                 pltpu.VMEM((3, fringe, LANES), F32),
-                dma((7,)),
-                dma((3,)),
+                dma((11,)),
                 dma((12,)),
                 dma((12,)),
                 dma((2, 2)),
                 dma((2, 2)),
                 dma((6,)),
                 dma((6,)),
+                pltpu.SemaphoreType.REGULAR((2,)),
             ],
             compiler_params=pltpu.CompilerParams(
                 collective_id=0, has_side_effects=True, vmem_limit_bytes=56 * 2**20
             ),
             cost_estimate=pl.CostEstimate(flops=flops, bytes_accessed=10**7, transcendentals=0),
-        )(fields, drag_here, weights, forward, inverse.astype(np.float32), lam.astype(np.float32))
+        )(
+            fields, drag_here, stream_gain, span_gain, wave, pick,
+            forward, inverse.astype(np.float32), lam.astype(np.float32),
+        )
         return out[None]
 
     return jax.shard_map(

time: 87.6 us -> 78.5 us (0.90)
  Pallas kernels: 82.4 us -> 77.3 us
  other arithmetic: 2.02 us -> 0 us
  local copies, waits for them, and re-layouts: 3.01 us -> 1.15 us
    pallas_call x1, Pallas kernels: 82.4 us -> 77.3 us  [shards(): pl.pallas_call(functools.partial(step_kernel, groups, sheets), name='frin...]
    unnamed x1, local copies, waits for them, and re-layouts: 2.67 us -> 1.15 us
    mul x2 -> x0, other arithmetic: 1.41 us -> none  [the longest x1 0.71 us: mode_weights(): stream_gain[:total_x // 2] * wave_x.astype(np.float32)]
where the time goes in v3:
time: 78.5 us; the launch traced here: 78.4 us
  Pallas kernels  77.3 us (98%)
  local copies, waits for them, and re-layouts  1.15 us (1%)
    pallas_call x1, Pallas kernels, shards(): pl.pallas_call(functools.partial(step_kernel, groups, sheets), name='frin...  77.3 us

profile of v3, /device:TPU:1, one launch (start us, length us, event | category | flops | bytes accessed | tf_op | source)
XLA Modules:
  0.0 78.4 jit_solution(13790164711362098732)
XLA Ops:
  0.0 77.3 %fringe_step.1 = f32[3,32,8,512]{3,2,1,0:T(8,128)S(1)} custom-call(f32[3,32,8,512]{3,2,1,0:T(8,128)} %bitcast.4, f32[32,8,512]{2,1,0:T(8,128)} %bitcast.5, f32[513]{0:T(1024)} %stream_hbm.1, f32[257]{0:T(512)} %span_hbm.1, f32[2,512]{1,0:T(2,128)} %constant.10.clone.wave_hbm, bf16[512,512]{1,0:T(8,128)(2,1)} %constant.11.clone.pick_hbm, ...), custom_call_target="tpu_custom_call" | custom-call | flops 8053063680 | bytes 10000000 | tf_op jit(solution)/shard_map/fringe_step/pallas_call | solution.py:365
  77.3 1.1 %copy.11 = f32[1,3,32,8,512]{4,3,2,1,0:T(8,128)} copy(f32[1,3,32,8,512]{4,3,2,1,0:T(8,128)S(1)} %bitcast.3) | data formatting | bytes 3145728

commit v4 on v3

--- a/solution.py
+++ b/solution.py
@@ -151,8 +151,7 @@
         pltpu.make_async_copy(wave_hbm, wave, load_sem.at[9]),
         pltpu.make_async_copy(pick_hbm, pick, load_sem.at[10]),
     ]
-    for load in loads:
-        load.start()
+    loads[0].start()
     barrier = pltpu.get_barrier_semaphore()
 
     def greet(k, carry):
@@ -168,6 +167,8 @@
     def _():
         pl.semaphore_signal(barrier, inc=1, device_id={"gz": gz + 1}, device_id_type=MESH)
 
+    loads[1].start()
+    loads[2].start()
     for c in range(3):
         loads[c].wait()
         for z in range(levels):
@@ -176,6 +177,8 @@
             pl.semaphore_wait(barrier, groups - 1 + jnp.minimum(gz, 1) + sec)
         to_pencils(v_here, 1, v_pen, c, c)
         if c == 0:
+            for load in loads[3:]:
+                load.start()
 
             @pl.when(gz > 0)
             def _():

time: 78.5 us -> 78.4 us (level)
  no operation moved by 1% of the time
where the time goes in v4:
time: 78.4 us; the launch traced here: 78.3 us
  Pallas kernels  77.1 us (98%)
  local copies, waits for them, and re-layouts  1.15 us (1%)
    pallas_call x1, Pallas kernels, shards(): pl.pallas_call(functools.partial(step_kernel, groups, sheets), name='frin...  77.1 us

profile of v4, /device:TPU:1, one launch (start us, length us, event | category | flops | bytes accessed | tf_op | source)
XLA Modules:
  0.0 78.3 jit_solution(12491483174482256385)
XLA Ops:
  0.0 77.1 %fringe_step.1 = f32[3,32,8,512]{3,2,1,0:T(8,128)S(1)} custom-call(f32[3,32,8,512]{3,2,1,0:T(8,128)} %bitcast.4, f32[32,8,512]{2,1,0:T(8,128)} %bitcast.5, f32[513]{0:T(1024)} %stream_hbm.1, f32[257]{0:T(512)} %span_hbm.1, f32[2,512]{1,0:T(2,128)} %constant.10.clone.wave_hbm, bf16[512,512]{1,0:T(8,128)(2,1)} %constant.11.clone.pick_hbm, ...), custom_call_target="tpu_custom_call" | custom-call | flops 8053063680 | bytes 10000000 | tf_op jit(solution)/shard_map/fringe_step/pallas_call | solution.py:368
  77.1 1.1 %copy.11 = f32[1,3,32,8,512]{4,3,2,1,0:T(8,128)} copy(f32[1,3,32,8,512]{4,3,2,1,0:T(8,128)S(1)} %bitcast.3) | data formatting | bytes 3145728
